TPU v7x, 256 devices: a whole 4x4x8 slice. The times are simulated.
256 devices in a mesh: fluid: 64 (over x, z, core), metal: 4 (over y).
Axes of the slice: x: 4, y: 4, z: 8, core: 2. Of those that a mesh axis runs over, the one named last changes fastest.
Arguments:
- fluid_x: bfloat16 [16384, 512], P('fluid', 'metal'), may hold values from -32 to 32
- metal_x: bfloat16 [8192, 512], P('fluid', 'metal'), may hold values from -32 to 32
- w_rf: bfloat16 [512, 512], P(None, 'metal'), may hold values from -0.5 to 0.5
- w_vf: bfloat16 [512, 512], P(None, 'metal'), may hold values from -0.25 to 0.25
- w_rm: bfloat16 [512, 512], P(None, 'metal'), may hold values from -0.5 to 0.5
- w_vm: bfloat16 [512, 512], P(None, 'metal'), may hold values from -0.25 to 0.25
- fluid_grad: bfloat16 [16384, 512], P('fluid', 'metal'), may hold values from -6 to 6
- metal_grad: bfloat16 [8192, 512], P('fluid', 'metal'), may hold values from -6 to 6
- pair_list: int32 [2048, 2], P('fluid'), may hold values from 0 to 63, as said below
- pair_count: int32 [64], P('fluid'), may hold values from 2 to 32, as said below
Outputs:
- fluid_out: bfloat16 [16384, 512], P('fluid', 'metal')
- metal_out: bfloat16 [8192, 512], P('fluid', 'metal')
- fluid_dx: bfloat16 [16384, 512], P('fluid', 'metal')
- metal_dx: bfloat16 [8192, 512], P('fluid', 'metal')
- weight_grads: float32 [4, 512, 512], P(None, None, 'metal')
Inputs may be any that keep to these rules, and one draw needn't show every extreme that they name: `pair_list`: column 0 is a local fluid block below 2, column 1 a metal block below 64. The first pair_count[d] entries of fluid index d are distinct pairs; every fluid block of every index and every metal block stands in some live entry; entries past the count hold valid indices and are ignored. `pair_count`: some fluid index has all 32 slots live.
All inputs are finite; a program needn't handle non-finite values.
Results may differ from a plain program's by a relative error of at most 0.0179.
The roundings to bfloat16 on the way count: a program that leaves them out, or rounds other values in their place, can miss the bound.
Values may be sent and summed in bfloat16 or wider, within the bound.
No kernel may reach another device: no remote copies, remote signals or barrier semaphores. Data moves between devices by JAX's collectives and lax.ppermute only.
A program may use at most 128 MiB of HBM per device.

v0:
```python
import math
import jax
import jax.numpy as jnp
from jax import lax
from jax.sharding import PartitionSpec as P

D = 512
H = 8
BLK = 128
LOWEST = -1e30


def project(inputs, weight):
    return jnp.dot(inputs, weight, preferred_element_type=jnp.float32).astype(jnp.bfloat16)


def back_project(grads, weight):
    return lax.dot_general(
        grads, weight, (((1,), (1,)), ((), ())), preferred_element_type=jnp.float32
    )


def outer_rows(inputs, grads):
    return lax.dot_general(
        inputs, grads, (((0,), (0,)), ((), ())), preferred_element_type=jnp.float32
    )


def body(fluid_x, metal_x, w_rf, w_vf, w_rm, w_vm, fluid_grad, metal_grad, pair_list, pair_count):
    head_size = D // H
    local_heads = w_rf.shape[1] // head_size
    feature_cols = w_rf.shape[1]
    fluid_rows = fluid_x.shape[0]
    blocks = fluid_rows // BLK
    metal_blocks = lax.axis_size("fluid")
    metal_rows = metal_blocks * BLK
    slot_total = pair_list.shape[0]
    batch_size = math.gcd(slot_total, 16)
    inv_root = 1.0 / math.sqrt(head_size)
    live_count = pair_count[0]
    loop_turns = slot_total // batch_size
    fluid_full, metal_full = (
        lax.all_gather(fluid_x, "metal", axis=1, tiled=True),
        lax.all_gather(metal_x, "metal", axis=1, tiled=True),
    )
    fluid_keys = project(fluid_full, w_rf)
    fluid_values = project(fluid_full, w_vf)
    metal_keys = project(metal_full, w_rm)
    metal_values = project(metal_full, w_vm)
    keys_all, values_all = (
        lax.all_gather(metal_keys, "fluid", axis=0, tiled=True),
        lax.all_gather(metal_values, "fluid", axis=0, tiled=True),
    )
    fkey_tiles = fluid_keys.reshape(blocks, BLK, local_heads, head_size)
    fval_tiles = fluid_values.reshape(blocks, BLK, local_heads, head_size)
    mkey_tiles = keys_all.reshape(metal_blocks, BLK, local_heads, head_size)
    mval_tiles = values_all.reshape(metal_blocks, BLK, local_heads, head_size)

    def batch_pairs(number):
        entries = lax.dynamic_slice_in_dim(pair_list, number * batch_size, batch_size, 0)
        slot_index = number * batch_size + jnp.arange(batch_size, dtype=jnp.int32)
        frows = entries[:, 0]
        mrows = entries[:, 1]
        scores = (
            jnp.einsum(
                "pahd,pbhd->phab",
                fkey_tiles[frows],
                mkey_tiles[mrows],
                preferred_element_type=jnp.float32,
            )
            * inv_root
        )
        return (frows, mrows, slot_index < live_count, scores)

    def max_pass(number, state):
        row_max, col_max = state
        frows, mrows, active, scores = batch_pairs(number)
        live = active[:, None, None]
        row_max = row_max.at[frows].max(jnp.where(live, jnp.max(scores, axis=3), LOWEST))
        col_max = col_max.at[mrows].max(jnp.where(live, jnp.max(scores, axis=2), LOWEST))
        return (row_max, col_max)

    row_max, col_local = lax.fori_loop(
        0,
        loop_turns,
        max_pass,
        (
            jnp.full((blocks, local_heads, BLK), LOWEST, jnp.float32),
            jnp.full((metal_blocks, local_heads, BLK), LOWEST, jnp.float32),
        ),
    )
    col_max = lax.pmax(col_local, "fluid")

    def sum_pass(number, state):
        row_sum, fluid_num, col_sum, metal_num = state
        frows, mrows, active, scores = batch_pairs(number)
        live = active[:, None, None, None]
        row_exp = jnp.where(live, jnp.exp(scores - row_max[frows][:, :, :, None]), 0.0)
        col_exp = jnp.where(live, jnp.exp(scores - col_max[mrows][:, :, None, :]), 0.0)
        row_sum = row_sum.at[frows].add(jnp.sum(row_exp, axis=3))
        col_sum = col_sum.at[mrows].add(jnp.sum(col_exp, axis=2))
        fluid_num = fluid_num.at[frows].add(
            jnp.einsum(
                "phab,pbhd->pahd",
                row_exp.astype(jnp.bfloat16),
                mval_tiles[mrows],
                preferred_element_type=jnp.float32,
            )
        )
        metal_num = metal_num.at[mrows].add(
            jnp.einsum(
                "phab,pahd->pbhd",
                col_exp.astype(jnp.bfloat16),
                fval_tiles[frows],
                preferred_element_type=jnp.float32,
            )
        )
        return (row_sum, fluid_num, col_sum, metal_num)

    row_sum, fluid_num, col_sum, metal_num = lax.fori_loop(
        0,
        loop_turns,
        sum_pass,
        (
            jnp.zeros((blocks, local_heads, BLK), jnp.float32),
            jnp.zeros((blocks, BLK, local_heads, head_size), jnp.float32),
            jnp.zeros((metal_blocks, local_heads, BLK), jnp.float32),
            jnp.zeros((metal_blocks, BLK, local_heads, head_size), jnp.float32),
        ),
    )
    fluid_out = (
        (fluid_num / row_sum.transpose(0, 2, 1)[:, :, :, None])
        .reshape(fluid_rows, feature_cols)
        .astype(jnp.bfloat16)
    )
    num_rows = metal_num.reshape(metal_rows, feature_cols)
    total_rows = col_sum.transpose(0, 2, 1).reshape(metal_rows, local_heads)
    own_num, own_sum = (
        lax.psum_scatter(num_rows, "fluid", scatter_dimension=0, tiled=True),
        lax.psum_scatter(total_rows, "fluid", scatter_dimension=0, tiled=True),
    )
    metal_out = (
        (own_num.reshape(BLK, local_heads, head_size) / own_sum[:, :, None])
        .reshape(BLK, feature_cols)
        .astype(jnp.bfloat16)
    )
    scaled_grad = (
        (metal_grad.astype(jnp.float32).reshape(BLK, local_heads, head_size) / own_sum[:, :, None])
        .reshape(BLK, feature_cols)
        .astype(jnp.bfloat16)
    )
    scaled_all, output_all = (
        lax.all_gather(scaled_grad, "fluid", axis=0, tiled=True),
        lax.all_gather(metal_out, "fluid", axis=0, tiled=True),
    )
    delta_f = jnp.sum(
        (fluid_grad.astype(jnp.float32) * fluid_out.astype(jnp.float32)).reshape(
            fluid_rows, local_heads, head_size
        ),
        axis=2,
    )
    delta_m = jnp.sum(
        (scaled_all.astype(jnp.float32) * output_all.astype(jnp.float32)).reshape(
            metal_blocks, BLK, local_heads, head_size
        ),
        axis=3,
    )
    grad_tiles = fluid_grad.reshape(blocks, BLK, local_heads, head_size)
    scaled_tiles = scaled_all.reshape(metal_blocks, BLK, local_heads, head_size)
    dfluid_tiles = delta_f.reshape(blocks, BLK, local_heads)

    def grad_pass(number, state):
        grad_rf, grad_vf, grad_rm, grad_vm = state
        frows, mrows, active, scores = batch_pairs(number)
        live = active[:, None, None, None]
        attn = jnp.where(
            live,
            jnp.exp(scores - row_max[frows][:, :, :, None]) / row_sum[frows][:, :, :, None],
            0.0,
        )
        col_exp = jnp.where(live, jnp.exp(scores - col_max[mrows][:, :, None, :]), 0.0)
        fluid_term = jnp.einsum(
            "pahd,pbhd->phab",
            grad_tiles[frows],
            mval_tiles[mrows],
            preferred_element_type=jnp.float32,
        )
        metal_term = jnp.einsum(
            "pahd,pbhd->phab",
            fval_tiles[frows],
            scaled_tiles[mrows],
            preferred_element_type=jnp.float32,
        )
        dscore = attn * (fluid_term - dfluid_tiles[frows].transpose(0, 2, 1)[:, :, :, None])
        dscore = dscore + col_exp * (metal_term - delta_m[mrows].transpose(0, 2, 1)[:, :, None, :])
        dscore_weight = dscore.astype(jnp.bfloat16)
        grad_rf = grad_rf.at[frows].add(
            jnp.einsum(
                "phab,pbhd->pahd",
                dscore_weight,
                mkey_tiles[mrows],
                preferred_element_type=jnp.float32,
            )
            * inv_root
        )
        grad_vf = grad_vf.at[frows].add(
            jnp.einsum(
                "phab,pbhd->pahd",
                col_exp.astype(jnp.bfloat16),
                scaled_tiles[mrows],
                preferred_element_type=jnp.float32,
            )
        )
        grad_rm = grad_rm.at[mrows].add(
            jnp.einsum(
                "phab,pahd->pbhd",
                dscore_weight,
                fkey_tiles[frows],
                preferred_element_type=jnp.float32,
            )
            * inv_root
        )
        grad_vm = grad_vm.at[mrows].add(
            jnp.einsum(
                "phab,pahd->pbhd",
                attn.astype(jnp.bfloat16),
                grad_tiles[frows],
                preferred_element_type=jnp.float32,
            )
        )
        return (grad_rf, grad_vf, grad_rm, grad_vm)

    grad_rf, grad_vf, grad_rm, grad_vm = lax.fori_loop(
        0,
        loop_turns,
        grad_pass,
        (
            jnp.zeros((blocks, BLK, local_heads, head_size), jnp.float32),
            jnp.zeros((blocks, BLK, local_heads, head_size), jnp.float32),
            jnp.zeros((metal_blocks, BLK, local_heads, head_size), jnp.float32),
            jnp.zeros((metal_blocks, BLK, local_heads, head_size), jnp.float32),
        ),
    )
    rf_rounded = grad_rf.reshape(fluid_rows, feature_cols).astype(jnp.bfloat16)
    vf_rounded = grad_vf.reshape(fluid_rows, feature_cols).astype(jnp.bfloat16)
    fluid_part = back_project(rf_rounded, w_rf) + back_project(vf_rounded, w_vf)
    fluid_part, weight_rf, weight_vf = (
        fluid_part,
        outer_rows(fluid_full, rf_rounded),
        outer_rows(fluid_full, vf_rounded),
    )
    rm_rounded = lax.psum_scatter(
        grad_rm.reshape(metal_rows, feature_cols), "fluid", scatter_dimension=0, tiled=True
    ).astype(jnp.bfloat16)
    vm_rounded = lax.psum_scatter(
        grad_vm.reshape(metal_rows, feature_cols), "fluid", scatter_dimension=0, tiled=True
    ).astype(jnp.bfloat16)
    metal_part = back_project(rm_rounded, w_rm) + back_project(vm_rounded, w_vm)
    weight_rm = outer_rows(metal_full, rm_rounded)
    weight_vm = outer_rows(metal_full, vm_rounded)
    fluid_dx, metal_dx = (
        lax.psum_scatter(fluid_part, "metal", scatter_dimension=1, tiled=True),
        lax.psum_scatter(metal_part, "metal", scatter_dimension=1, tiled=True),
    )
    weight_grads = lax.psum(jnp.stack([weight_rf, weight_vf, weight_rm, weight_vm]), "fluid")
    return (
        fluid_out,
        metal_out,
        fluid_dx.astype(jnp.bfloat16),
        metal_dx.astype(jnp.bfloat16),
        weight_grads,
    )


def solution(mesh):
    placed = (
        P("fluid", "metal"),
        P("fluid", "metal"),
        P(None, "metal"),
        P(None, "metal"),
        P(None, "metal"),
        P(None, "metal"),
        P("fluid", "metal"),
        P("fluid", "metal"),
        P("fluid", None),
        P("fluid"),
    )
    return jax.shard_map(
        body,
        mesh=mesh,
        in_specs=placed,
        out_specs=(
            P("fluid", "metal"),
            P("fluid", "metal"),
            P("fluid", "metal"),
            P("fluid", "metal"),
            P(None, None, "metal"),
        ),
        check_vma=False,
    )
```

profile of v0, /device:TPU:2, one launch (start us, length us, event | category | flops | bytes accessed | tf_op | source)
XLA Modules:
  0.0 1555.2 jit_solution(13822160661187020611)
XLA Ops:
  7.2 11.8 all_gather.19
  22.6 11.7 all_gather.18
  34.7 64.7 %all-gather.5.cloned.1.call-done = bf16[8192,128]{1,0:T(8,128)(2,1)} async-done(((bf16[128,128]{1,0:T(8,128)(2,1)}), bf16[8192,128]{1,0:T(8,128)(2,1)}) %all-gather.5.cloned.1.call-update) | async-done | bytes 2097168 | tf_op jit(solution)/shard_map/all_gather | solution.py:51
  99.4 8.2 reshape.334
  107.6 23.2 %while.53 = (s32[]{:T(128)}, f32[2,2,128]{2,1,0:T(2,128)S(1)}, f32[64,2,128]{2,1,0:T(2,128)S(1)}, s32[32,2]{0,1:T(2,128)S(1)}, s32[]{:T(128)}, /*index=5*/bf16[2...) while((s32[]{:T(128)}, f32[2,2,128]{2,1,0:T(2,128)S(1)}, ...), condition=%wide.region_5.6_spmd, body=%wide.region_0.5_spmd.sunk | while | flops 68692104 | bytes 3351623 | solution.py:83
  108.4 4.8 gather_fusion
  120.0 4.8 gather_fusion
  131.9 45.8 %all-gather.7.cloned.1.call-done = bf16[8192,128]{1,0:T(8,128)(2,1)} async-done(((bf16[128,128]{1,0:T(8,128)(2,1)}), bf16[8192,128]{1,0:T(8,128)(2,1)}) %all-gather.7.cloned.1.call-update) | async-done | bytes 2097168 | tf_op jit(solution)/shard_map/all_gather | solution.py:52
  177.7 8.3 reshape.335
  185.9 161.9 %all-reduce.3.cloned.1.call-done = f32[64,2,128]{2,1,0:T(2,128)} async-done(((f32[64,2,128]{2,1,0:T(2,128)}), f32[64,2,128]{2,1,0:T(2,128)}) %all-reduce.3.cloned.1.call-update) | async-done | bytes 65552 | tf_op jit(solution)/shard_map/pmax | solution.py:92
  350.3 67.5 %while.54 = (s32[]{:T(128)}, f32[2,2,128]{2,1,0:T(2,128)S(1)}, f32[2,128,2,64]{1,3,2,0:T(8,128)S(1)}, f32[64,2,128]{2,1,0:T(2,128)S(1)}, f32[64,128,2,64]{1,3,2,...) while((s32[]{:T(128)}, f32[2,2,128]{2,1,0:T(2,128)S(1)}, ...), condition=%wide.region_14.15_spmd, body=%wide.region_7.14_spmd.sunk | while | flops 209717376 | bytes 25437748 | solution.py:120
  353.3 4.8 gather_fusion.6
  358.2 5.7 gather_fusion.4
  386.7 4.8 gather_fusion.6
  391.6 5.7 gather_fusion.4
  425.2 5.2 copy.186
  431.3 130.0 %reduce-scatter.19.cloned.1.call-done = f32[128,2]{1,0:T(8,128)} async-done(((f32[8192,2]{1,0:T(8,128)}), f32[128,2]{1,0:T(8,128)}) %reduce-scatter.19.cloned.1.call-update) | async-done | bytes 1040
  562.2 145.2 %reduce-scatter.9.cloned.1.call-done = f32[128,128]{0,1:T(8,128)} async-done(((f32[8192,128]{0,1:T(8,128)}), f32[128,128]{0,1:T(8,128)}) %reduce-scatter.9.cloned.1.call-update) | async-done | bytes 65552 | tf_op jit(solution)/shard_map/reduce_scatter | solution.py:139
  710.1 72.3 %all-gather.9.cloned.1.call-done = bf16[8192,128]{0,1:T(8,128)(2,1)} async-done(((bf16[128,128]{0,1:T(8,128)(2,1)}), bf16[8192,128]{0,1:T(8,128)(2,1)}) %all-gather.9.cloned.1.call-update) | async-done | bytes 2097168 | tf_op jit(solution)/shard_map/all_gather | solution.py:153
  782.4 74.9 %all-gather.11.cloned.1.call-done = bf16[8192,128]{0,1:T(8,128)(2,1)} async-done(((bf16[128,128]{0,1:T(8,128)(2,1)}), bf16[8192,128]{0,1:T(8,128)(2,1)}) %all-gather.11.cloned.1.call-update) | async-done | bytes 2097168 | tf_op jit(solution)/shard_map/all_gather | solution.py:154
  867.4 5.2 copy.114
  877.5 131.7 %while.55 = (s32[]{:T(128)}, f32[2,128,2,64]{1,3,2,0:T(8,128)S(1)}, f32[2,128,2,64]{1,3,2,0:T(8,128)S(1)}, f32[64,128,2,64]{1,3,2,0:T(8,128)}, f32[64,128,2,64]{...) while((s32[]{:T(128)}, f32[2,128,2,64]{1,3,2,0:T(8,128)S(1)}, ...), condition=%wide.region_24.25_spmd, body=%wide.region_19.24_spmd.sunk | while | flops 482347136 | bytes 61189336 | solution.py:233
  895.4 5.7 gather_fusion.8
  949.6 4.8 gather_fusion.11
  961.1 5.7 gather_fusion.8
  1013.9 5.2 copy.184
  1023.8 5.3 copy.185
  1031.5 129.8 %reduce-scatter.15.cloned.1.call-done = f32[128,128]{0,1:T(8,128)} async-done(((f32[8192,128]{0,1:T(8,128)}), f32[128,128]{0,1:T(8,128)}) %reduce-scatter.15.cloned.1.call-update) | async-done | bytes 65552 | tf_op jit(solution)/shard_map/reduce_scatter | solution.py:255
  1162.3 145.3 %reduce-scatter.13.cloned.1.call-done = f32[128,128]{0,1:T(8,128)} async-done(((f32[8192,128]{0,1:T(8,128)}), f32[128,128]{0,1:T(8,128)}) %reduce-scatter.13.cloned.1.call-update) | async-done | bytes 65552 | tf_op jit(solution)/shard_map/reduce_scatter | solution.py:252
  1312.6 20.7 %reduce-scatter.11.cloned.1.call-done = f32[256,128]{1,0:T(8,128)} async-done(((f32[256,512]{1,0:T(8,128)}), f32[256,128]{1,0:T(8,128)}) %reduce-scatter.11.cloned.1.call-update) | async-done | bytes 131088 | tf_op jit(solution)/shard_map/reduce_scatter | solution.py:262
  1334.8 188.6 %all-reduce.5.cloned.1.call-done = f32[4,512,128]{1,2,0:T(8,128)} async-done(((f32[4,512,128]{1,2,0:T(8,128)}), f32[4,512,128]{1,2,0:T(8,128)}) %all-reduce.5.cloned.1.call-update) | async-done | bytes 1048592 | tf_op jit(solution)/shard_map/psum | solution.py:265
  1525.9 20.6 %reduce-scatter.17.cloned.1.call-done = f32[128,128]{1,0:T(8,128)} async-done(((f32[128,512]{1,0:T(8,128)}), f32[128,128]{1,0:T(8,128)}) %reduce-scatter.17.cloned.1.call-update) | async-done | bytes 65552 | tf_op jit(solution)/shard_map/reduce_scatter | solution.py:263
  (261 shorter events, 230.9 us)
Async XLA Ops:
  7.2 27.2 %copy-start = (bf16[512,128]{1,0:T(8,128)(2,1)S(1)}, bf16[512,128]{1,0:T(8,128)(2,1)}, u32[]{:S(2)}) copy-start(bf16[512,128]{1,0:T(8,128)(2,1)} %param.18) | copy-start | bytes 393220
  7.2 92.2 %all-gather.5.cloned.1.call-start = ((), (), s32[]{:S(2)}) async-start(), calls=%async_computation.6 | async-start | bytes 2129920 | tf_op jit(solution)/shard_map/all_gather | solution.py:51
  19.0 15.3 copy-start.8
  20.8 156.9 %all-gather.7.cloned.1.call-start = ((), (), s32[]{:S(2)}) async-start(), calls=%async_computation.7 | async-start | bytes 2129920 | tf_op jit(solution)/shard_map/all_gather | solution.py:52
  22.6 325.3 %all-reduce.3.cloned.1.call-start = ((), (), s32[]{:S(2)}) async-start(), calls=%async_computation.8 | async-start | bytes 131072 | tf_op jit(solution)/shard_map/pmax | solution.py:92
  34.3 97.2 %copy-start.6 = (bf16[256,512]{1,0:T(8,128)(2,1)}, bf16[256,512]{1,0:T(8,128)(2,1)S(1)}, u32[]{:S(2)}) copy-start(bf16[256,512]{1,0:T(8,128)(2,1)S(1)} %all_gather.18) | copy-start | bytes 786436
  34.7 72.9 %copy-start.22 = (s32[32,2]{0,1:T(2,128)S(1)}, s32[32,2]{0,1:T(2,128)}, u32[]{:S(2)}) copy-start(s32[32,2]{0,1:T(2,128)} %param.24) | copy-start | bytes 772
  107.6 24.0 %copy-start.13 = (bf16[512,128]{1,0:T(8,128)(2,1)S(1)}, bf16[512,128]{1,0:T(8,128)(2,1)}, u32[]{:S(2)}) copy-start(bf16[512,128]{1,0:T(8,128)(2,1)} %param.19) | copy-start | bytes 393220
  131.5 429.8 %reduce-scatter.19.cloned.1.call-start = ((), (), s32[]{:S(2)}) async-start(), calls=%async_computation.17 | async-start | bytes 4259840
  376.7 3.9 copy-start.1
  410.1 3.9 copy-start.1
  420.5 286.9 %reduce-scatter.9.cloned.1.call-start = ((), (), s32[]{:S(2)}) async-start(), calls=%async_computation.9 | async-start | bytes 4259840 | tf_op jit(solution)/shard_map/reduce_scatter | solution.py:139
  430.4 279.3 %copy-start.20 = (bf16[256,128]{1,0:T(8,128)(2,1)S(1)}, bf16[256,128]{1,0:T(8,128)(2,1)}, u32[]{:S(2)}) copy-start(bf16[256,128]{1,0:T(8,128)(2,1)} %param.22) | copy-start | bytes 196612
  430.5 351.9 %all-gather.9.cloned.1.call-start = ((), (), s32[]{:S(2)}) async-start(), calls=%async_computation.10 | async-start | bytes 2129920 | tf_op jit(solution)/shard_map/all_gather | solution.py:153
  708.9 148.3 %all-gather.11.cloned.1.call-start = ((), (), s32[]{:S(2)}) async-start(), calls=%async_computation.11 | async-start | bytes 2129920 | tf_op jit(solution)/shard_map/all_gather | solution.py:154
  709.7 451.6 %reduce-scatter.15.cloned.1.call-start = ((), (), s32[]{:S(2)}) async-start(), calls=%async_computation.14 | async-start | bytes 4259840 | tf_op jit(solution)/shard_map/reduce_scatter | solution.py:255
  710.0 149.9 %copy-start.11 = (bf16[2,128,2,64]{1,0,3,2:T(2,128)(2,1)}, bf16[2,128,2,64]{1,0,3,2:T(2,128)(2,1)S(1)}, u32[]{:S(2)}) copy-start(bf16[2,128,2,64]{1,0,3,2:T(2,128)(2,1)S(1)} %copy.104) | copy-start | bytes 196612
  933.9 2.6 copy-start.2
  933.9 2.6 copy-start.24
  936.5 3.4 copy-start.5
  999.6 2.6 copy-start.2
  999.6 2.6 copy-start.24
  1002.2 3.4 copy-start.5
  1019.1 288.5 %reduce-scatter.13.cloned.1.call-start = ((), (), s32[]{:S(2)}) async-start(), calls=%async_computation.13 | async-start | bytes 4259840 | tf_op jit(solution)/shard_map/reduce_scatter | solution.py:252
  1029.1 304.2 %reduce-scatter.11.cloned.1.call-start = ((), (), s32[]{:S(2)}) async-start(), calls=%async_computation.12 | async-start | bytes 655360 | tf_op jit(solution)/shard_map/reduce_scatter | solution.py:262
  1029.1 132.1 %copy-start.9 = (bf16[128,512]{1,0:T(8,128)(2,1)S(1)}, bf16[128,512]{1,0:T(8,128)(2,1)}, u32[]{:S(2)}) copy-start(bf16[128,512]{1,0:T(8,128)(2,1)} %copy-done.8) | copy-start | bytes 393220
  1031.0 492.3 %all-reduce.5.cloned.1.call-start = ((), (), s32[]{:S(2)}) async-start(), calls=%async_computation.16 | async-start | bytes 2097152 | tf_op jit(solution)/shard_map/psum | solution.py:265
  1031.5 278.4 %copy-start.15 = (bf16[512,128]{1,0:T(8,128)(2,1)S(1)}, bf16[512,128]{1,0:T(8,128)(2,1)}, u32[]{:S(2)}) copy-start(bf16[512,128]{1,0:T(8,128)(2,1)} %param.20) | copy-start | bytes 393220
  1162.3 147.8 %copy-start.16 = (bf16[512,128]{1,0:T(8,128)(2,1)S(1)}, bf16[512,128]{1,0:T(8,128)(2,1)}, u32[]{:S(2)}) copy-start(bf16[512,128]{1,0:T(8,128)(2,1)} %param.21) | copy-start | bytes 393220
  1162.3 147.8 %copy-start.21 = (f32[128,128]{0,1:T(8,128)S(1)}, f32[128,128]{0,1:T(8,128)}, u32[]{:S(2)}) copy-start(f32[128,128]{0,1:T(8,128)} %reduce-scatter.15.cloned.1.call-done) | copy-start | bytes 196612
  1308.7 3.1 copy-start.18
  1309.8 236.7 %reduce-scatter.17.cloned.1.call-start = ((), (), s32[]{:S(2)}) async-start(), calls=%async_computation.15 | async-start | bytes 327680 | tf_op jit(solution)/shard_map/reduce_scatter | solution.py:263
  (20 other events, 25.4 us)
Sparse Core Ops, SparseCore 0:
  20.9 78.4 all-gather.4
  102.7 74.9 all-gather.6
  181.8 166.0 all-reduce.2
  420.7 140.5 reduce-scatter.18
  565.3 142.0 reduce-scatter.8
  710.7 71.6 all-gather.8
  785.8 71.3 all-gather.10
  1019.2 141.9 reduce-scatter.14
  1165.4 142.1 reduce-scatter.12
  1310.2 23.0 reduce-scatter.10
  1337.7 185.6 all-reduce.4
  1525.7 20.7 reduce-scatter.16
where the time goes:
time: 1570 us; the launch traced here: 1560 us
  waiting for transfers between devices  1200 us (76%)
  local copies, waits for them, and re-layouts  209 us (13%)
  other arithmetic  58.9 us (4%)
  matrix products  46.7 us (3%)
  blocking collectives  23.5 us (1%)
    psum x1, waiting for transfers between devices, body(): lax.psum(jnp.stack([weight_rf, weight_vf, weight_rm, weight_vm]), 'fluid')  189 us
    pmax x1, waiting for transfers between devices, body(): col_max = lax.pmax(col_local, 'fluid')  162 us
    reduce_scatter x1, waiting for transfers between devices, body(): lax.psum_scatter(grad_rm.reshape(metal_rows, feature_cols), 'fluid', scat...  145 us
    reduce_scatter x1, waiting for transfers between devices, body(): lax.psum_scatter(num_rows, 'fluid', scatter_dimension=0, tiled=True)  145 us
    unnamed x13, waiting for transfers between devices  131 us
    reduce_scatter x1, waiting for transfers between devices, body(): lax.psum_scatter(grad_vm.reshape(metal_rows, feature_cols), 'fluid', scat...  130 us
    all_gather x1, waiting for transfers between devices, body(): lax.all_gather(metal_out, 'fluid', axis=0, tiled=True)  74.9 us
    all_gather x1, waiting for transfers between devices, body(): lax.all_gather(scaled_grad, 'fluid', axis=0, tiled=True)  72.3 us
  transfers between devices with their start and end apart: 12, of which 12 were waited for; matrix products, arithmetic and copies ran while one was open for 5% of the time, Pallas kernels for 0%

commit v1 on v0

--- a/solution.py
+++ b/solution.py
@@ -262,7 +262,9 @@
         lax.psum_scatter(fluid_part, "metal", scatter_dimension=1, tiled=True),
         lax.psum_scatter(metal_part, "metal", scatter_dimension=1, tiled=True),
     )
-    weight_grads = lax.psum(jnp.stack([weight_rf, weight_vf, weight_rm, weight_vm]), "fluid")
+    weight_grads = jnp.sum(
+        lax.all_gather(jnp.stack([weight_rf, weight_vf, weight_rm, weight_vm]), "fluid"), axis=0
+    )
     return (
         fluid_out,
         metal_out,

time: 1570 us -> 1640 us (1.045)
  waiting for transfers between devices: 1200 us -> 1240 us
  other arithmetic: 58.9 us -> 83 us
    all_gather x0 -> x1, waiting for transfers between devices: none -> 237 us  [body(): lax.all_gather(jnp.stack([weight_rf, weight_vf, weight_rm, weight_vm]), '...]
    psum x1 -> x0, waiting for transfers between devices: 189 us -> none  [body(): lax.psum(jnp.stack([weight_rf, weight_vf, weight_rm, weight_vm]), 'fluid')]
    reduce_sum x0 -> x1, other arithmetic: none -> 21.7 us  [body(): jnp.sum(lax.all_gather(jnp.stack([weight_rf, weight_vf, weight_rm, weight...]
where the time goes in v1:
time: 1640 us; the launch traced here: 1630 us
  waiting for transfers between devices  1240 us (76%)
  local copies, waits for them, and re-layouts  197 us (12%)
  other arithmetic  83 us (5%)
  matrix products  62.6 us (4%)
  blocking collectives  23.5 us (1%)
    all_gather x1, waiting for transfers between devices, body(): lax.all_gather(jnp.stack([weight_rf, weight_vf, weight_rm, weight_vm]), '...  237 us
    pmax x1, waiting for transfers between devices, body(): col_max = lax.pmax(col_local, 'fluid')  162 us
    reduce_scatter x1, waiting for transfers between devices, body(): lax.psum_scatter(num_rows, 'fluid', scatter_dimension=0, tiled=True)  145 us
    reduce_scatter x1, waiting for transfers between devices, body(): lax.psum_scatter(grad_vm.reshape(metal_rows, feature_cols), 'fluid', scat...  145 us
    unnamed x13, waiting for transfers between devices  131 us
    reduce_scatter x1, waiting for transfers between devices, body(): lax.psum_scatter(grad_rm.reshape(metal_rows, feature_cols), 'fluid', scat...  130 us
    all_gather x1, waiting for transfers between devices, body(): lax.all_gather(scaled_grad, 'fluid', axis=0, tiled=True)  72.3 us
    all_gather x1, waiting for transfers between devices, body(): lax.all_gather(metal_out, 'fluid', axis=0, tiled=True)  67.5 us
  transfers between devices with their start and end apart: 12, of which 12 were waited for; matrix products, arithmetic and copies ran while one was open for 5% of the time, Pallas kernels for 0%

profile of v1, /device:TPU:2, one launch (start us, length us, event | category | flops | bytes accessed | tf_op | source)
XLA Modules:
  0.0 1627.5 jit_solution(9833254035275752713)
XLA Ops:
  7.2 11.8 all_gather.25
  22.6 11.7 all_gather.24
  34.7 64.7 %all-gather.7.cloned.1.call-done = bf16[8192,128]{1,0:T(8,128)(2,1)} async-done(((bf16[128,128]{1,0:T(8,128)(2,1)}), bf16[8192,128]{1,0:T(8,128)(2,1)}) %all-gather.7.cloned.1.call-update) | async-done | bytes 2097168 | tf_op jit(solution)/shard_map/all_gather | solution.py:51
  99.4 8.2 reshape.335
  107.6 23.2 %while.53 = (s32[]{:T(128)}, f32[2,2,128]{2,1,0:T(2,128)S(1)}, f32[64,2,128]{2,1,0:T(2,128)S(1)}, s32[32,2]{0,1:T(2,128)S(1)}, s32[]{:T(128)}, /*index=5*/bf16[2...) while((s32[]{:T(128)}, f32[2,2,128]{2,1,0:T(2,128)S(1)}, ...), condition=%wide.region_5.6_spmd, body=%wide.region_0.5_spmd.sunk | while | flops 68692104 | bytes 3351631 | solution.py:83
  119.3 4.8 gather_fusion
  131.9 45.8 %all-gather.9.cloned.1.call-done = bf16[8192,128]{1,0:T(8,128)(2,1)} async-done(((bf16[128,128]{1,0:T(8,128)(2,1)}), bf16[8192,128]{1,0:T(8,128)(2,1)}) %all-gather.9.cloned.1.call-update) | async-done | bytes 2097168 | tf_op jit(solution)/shard_map/all_gather | solution.py:52
  177.7 8.3 reshape.336
  186.0 161.9 %all-reduce.2.cloned.1.call-done = f32[64,2,128]{2,1,0:T(2,128)} async-done(((f32[64,2,128]{2,1,0:T(2,128)}), f32[64,2,128]{2,1,0:T(2,128)}) %all-reduce.2.cloned.1.call-update) | async-done | bytes 65552 | tf_op jit(solution)/shard_map/pmax | solution.py:92
  350.4 79.8 %while.54 = (s32[]{:T(128)}, f32[2,2,128]{2,1,0:T(2,128)S(1)}, f32[2,128,2,64]{1,3,2,0:T(8,128)S(1)}, f32[64,2,128]{2,1,0:T(2,128)S(1)}, f32[64,128,2,64]{1,3,2,...) while((s32[]{:T(128)}, f32[2,2,128]{2,1,0:T(2,128)S(1)}, ...), condition=%wide.region_14.15_spmd, body=%wide.region_7.14_spmd.sunk | while | flops 209717376 | bytes 21243424 | solution.py:120
  353.3 5.7 gather_fusion.4
  367.0 5.7 gather_fusion.6
  392.9 5.7 gather_fusion.4
  406.6 5.7 gather_fusion.6
  437.5 5.2 copy.187
  443.6 130.1 %reduce-scatter.19.cloned.1.call-done = f32[128,2]{1,0:T(8,128)} async-done(((f32[8192,2]{1,0:T(8,128)}), f32[128,2]{1,0:T(8,128)}) %reduce-scatter.19.cloned.1.call-update) | async-done | bytes 1040
  574.5 145.3 %reduce-scatter.9.cloned.1.call-done = f32[128,128]{0,1:T(8,128)} async-done(((f32[8192,128]{0,1:T(8,128)}), f32[128,128]{0,1:T(8,128)}) %reduce-scatter.9.cloned.1.call-update) | async-done | bytes 65552 | tf_op jit(solution)/shard_map/reduce_scatter | solution.py:139
  722.5 72.3 %all-gather.11.cloned.1.call-done = bf16[8192,128]{0,1:T(8,128)(2,1)} async-done(((bf16[128,128]{0,1:T(8,128)(2,1)}), bf16[8192,128]{0,1:T(8,128)(2,1)}) %all-gather.11.cloned.1.call-update) | async-done | bytes 2097168 | tf_op jit(solution)/shard_map/all_gather | solution.py:153
  797.0 5.2 copy.112
  802.1 67.5 %all-gather.13.cloned.1.call-done = bf16[8192,128]{0,1:T(8,128)(2,1)} async-done(((bf16[128,128]{0,1:T(8,128)(2,1)}), bf16[8192,128]{0,1:T(8,128)(2,1)}) %all-gather.13.cloned.1.call-update) | async-done | bytes 2097168 | tf_op jit(solution)/shard_map/all_gather | solution.py:154
  882.5 128.4 %while.55 = (s32[]{:T(128)}, f32[2,128,2,64]{1,3,2,0:T(8,128)S(1)}, f32[2,128,2,64]{1,3,2,0:T(8,128)S(1)}, f32[64,128,2,64]{1,3,2,0:T(8,128)}, f32[64,128,2,64]{...) while((s32[]{:T(128)}, f32[2,128,2,64]{1,3,2,0:T(8,128)S(1)}, ...), condition=%wide.region_24.25_spmd, body=%wide.region_19.24_spmd.sunk | while | flops 482347136 | bytes 61191380 | solution.py:233
  882.8 4.8 gather_fusion.8
  891.7 5.0 gather_fusion.10
  955.8 5.0 gather_fusion.10
  1015.6 5.2 copy.186
  1025.5 5.3 copy.185
  1032.8 130.1 %reduce-scatter.13.cloned.1.call-done = f32[128,128]{0,1:T(8,128)} async-done(((f32[8192,128]{0,1:T(8,128)}), f32[128,128]{0,1:T(8,128)}) %reduce-scatter.13.cloned.1.call-update) | async-done | bytes 65552 | tf_op jit(solution)/shard_map/reduce_scatter | solution.py:252
  1164.0 145.1 %reduce-scatter.15.cloned.1.call-done = f32[128,128]{0,1:T(8,128)} async-done(((f32[8192,128]{0,1:T(8,128)}), f32[128,128]{0,1:T(8,128)}) %reduce-scatter.15.cloned.1.call-update) | async-done | bytes 65552 | tf_op jit(solution)/shard_map/reduce_scatter | solution.py:255
  1314.8 20.2 %reduce-scatter.11.cloned.1.call-done = f32[256,128]{1,0:T(8,128)} async-done(((f32[256,512]{1,0:T(8,128)}), f32[256,128]{1,0:T(8,128)}) %reduce-scatter.11.cloned.1.call-update) | async-done | bytes 131088 | tf_op jit(solution)/shard_map/reduce_scatter | solution.py:262
  1336.5 24.0 %reduce-scatter.17.cloned.1.call-done = f32[128,128]{1,0:T(8,128)} async-done(((f32[128,512]{1,0:T(8,128)}), f32[128,128]{1,0:T(8,128)}) %reduce-scatter.17.cloned.1.call-update) | async-done | bytes 65552 | tf_op jit(solution)/shard_map/reduce_scatter | solution.py:263
  1362.0 236.6 %all-gather.15.cloned.1.call-done = f32[256,512,128]{2,1,0:T(8,128)} async-done(((f32[4,512,128]{2,1,0:T(8,128)}), f32[256,512,128]{2,1,0:T(8,128)}) %all-gather.15.cloned.1.call-update) | async-done | bytes 67108880 | tf_op jit(solution)/shard_map/all_gather | solution.py:266
  1598.6 21.7 %reduce_sum.55 = f32[4,512,128]{2,1,0:T(8,128)} reduce(f32[64,4,512,128]{3,2,1,0:T(8,128)} %bitcast.29, f32[]{:T(128)} %constant.175.clone.1), dimensions={0}, to_apply=%region_29.30 | reduce | flops 16515072 | bytes 68157440 | tf_op jit(solution)/shard_map/reduce_sum | solution.py:265
  (266 shorter events, 242.0 us)
Async XLA Ops:
  7.2 27.2 %copy-start = (bf16[512,128]{1,0:T(8,128)(2,1)S(1)}, bf16[512,128]{1,0:T(8,128)(2,1)}, u32[]{:S(2)}) copy-start(bf16[512,128]{1,0:T(8,128)(2,1)} %param.18) | copy-start | bytes 393220
  7.2 92.2 %all-gather.7.cloned.1.call-start = ((), (), s32[]{:S(2)}) async-start(), calls=%async_computation.6 | async-start | bytes 2129920 | tf_op jit(solution)/shard_map/all_gather | solution.py:51
  19.0 15.3 copy-start.8
  20.8 156.9 %all-gather.9.cloned.1.call-start = ((), (), s32[]{:S(2)}) async-start(), calls=%async_computation.7 | async-start | bytes 2129920 | tf_op jit(solution)/shard_map/all_gather | solution.py:52
  22.6 325.3 %all-reduce.2.cloned.1.call-start = ((), (), s32[]{:S(2)}) async-start(), calls=%async_computation.8 | async-start | bytes 131072 | tf_op jit(solution)/shard_map/pmax | solution.py:92
  34.3 97.2 %copy-start.6 = (bf16[256,512]{1,0:T(8,128)(2,1)}, bf16[256,512]{1,0:T(8,128)(2,1)S(1)}, u32[]{:S(2)}) copy-start(bf16[256,512]{1,0:T(8,128)(2,1)S(1)} %all_gather.24) | copy-start | bytes 786436
  34.7 72.9 %copy-start.22 = (s32[32,2]{0,1:T(2,128)S(1)}, s32[32,2]{0,1:T(2,128)}, u32[]{:S(2)}) copy-start(s32[32,2]{0,1:T(2,128)} %param.24) | copy-start | bytes 772
  107.6 23.9 %copy-start.13 = (bf16[512,128]{1,0:T(8,128)(2,1)S(1)}, bf16[512,128]{1,0:T(8,128)(2,1)}, u32[]{:S(2)}) copy-start(bf16[512,128]{1,0:T(8,128)(2,1)} %param.19) | copy-start | bytes 393220
  131.5 442.1 %reduce-scatter.19.cloned.1.call-start = ((), (), s32[]{:S(2)}) async-start(), calls=%async_computation.17 | async-start | bytes 4259840
  432.8 287.0 %reduce-scatter.9.cloned.1.call-start = ((), (), s32[]{:S(2)}) async-start(), calls=%async_computation.9 | async-start | bytes 4259840 | tf_op jit(solution)/shard_map/reduce_scatter | solution.py:139
  442.7 279.4 %copy-start.20 = (bf16[256,128]{1,0:T(8,128)(2,1)S(1)}, bf16[256,128]{1,0:T(8,128)(2,1)}, u32[]{:S(2)}) copy-start(bf16[256,128]{1,0:T(8,128)(2,1)} %param.22) | copy-start | bytes 196612
  442.7 352.1 %all-gather.11.cloned.1.call-start = ((), (), s32[]{:S(2)}) async-start(), calls=%async_computation.10 | async-start | bytes 2129920 | tf_op jit(solution)/shard_map/all_gather | solution.py:153
  721.3 148.4 %all-gather.13.cloned.1.call-start = ((), (), s32[]{:S(2)}) async-start(), calls=%async_computation.11 | async-start | bytes 2129920 | tf_op jit(solution)/shard_map/all_gather | solution.py:154
  722.0 440.9 %reduce-scatter.13.cloned.1.call-start = ((), (), s32[]{:S(2)}) async-start(), calls=%async_computation.13 | async-start | bytes 4259840 | tf_op jit(solution)/shard_map/reduce_scatter | solution.py:252
  722.4 72.4 %copy-start.11 = (bf16[2,128,2,64]{1,0,3,2:T(2,128)(2,1)}, bf16[2,128,2,64]{1,0,3,2:T(2,128)(2,1)S(1)}, u32[]{:S(2)}) copy-start(bf16[2,128,2,64]{1,0,3,2:T(2,128)(2,1)S(1)} %copy.102) | copy-start | bytes 196612
  882.7 5.7 copy-start.23
  882.8 8.2 copy-start.25
  882.8 8.2 copy-start.27
  891.7 7.3 copy-start.3
  946.7 5.6 copy-start.23
  946.8 8.2 copy-start.25
  946.8 8.2 copy-start.27
  955.8 7.3 copy-start.3
  1020.8 288.4 %reduce-scatter.15.cloned.1.call-start = ((), (), s32[]{:S(2)}) async-start(), calls=%async_computation.14 | async-start | bytes 4259840 | tf_op jit(solution)/shard_map/reduce_scatter | solution.py:255
  1030.8 132.1 %copy-start.15 = (bf16[512,128]{1,0:T(8,128)(2,1)S(1)}, bf16[512,128]{1,0:T(8,128)(2,1)}, u32[]{:S(2)}) copy-start(bf16[512,128]{1,0:T(8,128)(2,1)} %param.20) | copy-start | bytes 393220
  1030.8 278.4 %copy-start.16 = (bf16[512,128]{1,0:T(8,128)(2,1)S(1)}, bf16[512,128]{1,0:T(8,128)(2,1)}, u32[]{:S(2)}) copy-start(bf16[512,128]{1,0:T(8,128)(2,1)} %param.21) | copy-start | bytes 393220
  1030.8 304.2 %reduce-scatter.11.cloned.1.call-start = ((), (), s32[]{:S(2)}) async-start(), calls=%async_computation.12 | async-start | bytes 655360 | tf_op jit(solution)/shard_map/reduce_scatter | solution.py:262
  1030.9 280.2 %copy-start.7 = (bf16[256,512]{1,0:T(8,128)(2,1)S(1)}, bf16[256,512]{1,0:T(8,128)(2,1)}, u32[]{:S(2)}) copy-start(bf16[256,512]{1,0:T(8,128)(2,1)} %copy-done.6) | copy-start | bytes 786436
  1031.6 279.9 %copy-start.9 = (bf16[128,512]{1,0:T(8,128)(2,1)S(1)}, bf16[128,512]{1,0:T(8,128)(2,1)}, u32[]{:S(2)}) copy-start(bf16[128,512]{1,0:T(8,128)(2,1)} %copy-done.8) | copy-start | bytes 393220
  1032.7 327.8 %reduce-scatter.17.cloned.1.call-start = ((), (), s32[]{:S(2)}) async-start(), calls=%async_computation.15 | async-start | bytes 327680 | tf_op jit(solution)/shard_map/reduce_scatter | solution.py:263
  1162.9 148.8 %copy-start.19 = (f32[128,128]{0,1:T(8,128)S(1)}, f32[128,128]{0,1:T(8,128)}, u32[]{:S(2)}) copy-start(f32[128,128]{0,1:T(8,128)} %reduce-scatter.13.cloned.1.call-done) | copy-start | bytes 196612
  1311.1 287.5 %all-gather.15.cloned.1.call-start = ((), (), s32[]{:S(2)}) async-start(), calls=%async_computation.16 | async-start | bytes 68157440 | tf_op jit(solution)/shard_map/all_gather | solution.py:266
  (22 other events, 52.3 us)
Sparse Core Ops, SparseCore 0:
  20.9 78.4 all-gather.6
  102.7 74.9 all-gather.8
  181.8 166.0 all-reduce.1
  432.9 140.6 reduce-scatter.18
  577.6 142.1 reduce-scatter.8
  723.1 71.6 all-gather.10
  798.2 71.3 all-gather.12
  1020.9 141.9 reduce-scatter.12
  1167.0 142.0 reduce-scatter.14
  1311.7 23.1 reduce-scatter.10
  1337.6 22.8 reduce-scatter.16
  1363.8 234.7 all-gather.14
